TPU v7x, 512 devices: a whole 4x4x16 slice. The times are simulated.
512 devices in a mesh: row: 128 (over z_lo, x, y, core), rep: 4 (over z_hi).
Axes of the slice: x: 4, y: 4, z: 16 (z_hi: 4, z_lo: 4; z = z_hi * 4 + z_lo), core: 2. Of those that a mesh axis runs over, the one named last changes fastest.
Arguments:
- grad_out: bfloat16 [65536, 256], P(('row', 'rep')), may hold values from -6 to 6
- pre_act: bfloat16 [65536, 256], P(('row', 'rep')), may hold values from -8 to 8
- features: bfloat16 [65536, 256], P(('row', 'rep')), may hold values from -6 to 6
- weight: bfloat16 [256, 256], replicated, may hold values from -0.375 to 0.375
- tile_values: bfloat16 [128, 4, 48, 128, 128], P('row', 'rep'), may hold values from -2.5 to 2.5
- tile_rows: int32 [128, 4, 48], P('row', 'rep'), may hold values from 0 to 3
- tile_cols: int32 [128, 4, 48], P('row', 'rep'), may hold values from 0 to 127
- tile_count: int32 [128, 4], P('row', 'rep'), may hold values from 6 to 48, as said below
- degrees: int32 [65536], P(('row', 'rep')), may hold values from 1 to 64
Outputs:
- grad_features: bfloat16 [65536, 256], P(('row', 'rep'))
- grad_weight: float32 [256, 256], replicated
Inputs may be any that keep to these rules, and one draw needn't show every extreme that they name: `tile_count`: slot counts of a device; some device uses all 48 slots.
All inputs are finite; a program needn't handle non-finite values.
Results may differ from a plain program's by a relative error of at most 0.015.
Values may be sent and summed in bfloat16 or wider, within the bound.
A program may use at most 64 MiB of HBM per device.

v0:
```python
import math

import jax
import jax.numpy as jnp
from jax import lax
from jax.sharding import PartitionSpec as P


def per_device(
    grad_out, pre_act, features, weight, tile_values, tile_rows, tile_cols, tile_count, degrees
):
    inv_sqrt = lax.rsqrt(degrees.astype(jnp.float32))[:, None]
    preact = pre_act.astype(jnp.float32)
    gate_sig = jax.nn.sigmoid(preact)
    grad_pre = grad_out.astype(jnp.float32) * gate_sig * (1.0 + preact * (1.0 - gate_sig))
    scaled_grad = (inv_sqrt * grad_pre).astype(jnp.bfloat16)
    block_rows, feat_width = scaled_grad.shape
    rep_count = lax.axis_size("rep")
    gathered = lax.all_gather(scaled_grad, "row", axis=0, tiled=True)
    column_blocks = gathered.reshape(-1, block_rows, feat_width)
    tile_vals = tile_values[0, 0]
    slot_total = tile_vals.shape[0]
    live_slots = jnp.arange(slot_total) < tile_count[0, 0]
    row_hot = (
        (tile_rows[0, 0][:, None] == jnp.arange(rep_count)[None, :]) & live_slots[:, None]
    ).astype(jnp.float32)
    col_index = tile_cols[0, 0]
    group_size = math.gcd(slot_total, 16)

    def add_group(group_idx, running):
        first_slot = group_idx * group_size
        group_tiles = lax.dynamic_slice_in_dim(tile_vals, first_slot, group_size, 0)
        group_cols = lax.dynamic_slice_in_dim(col_index, first_slot, group_size, 0)
        picked = jnp.take(column_blocks, group_cols, axis=0)
        product = jnp.einsum(
            "sij,sjf->sif", group_tiles, picked, preferred_element_type=jnp.float32
        )
        hot_rows = lax.dynamic_slice_in_dim(row_hot, first_slot, group_size, 0)
        return running + jnp.einsum("sr,sif->rif", hot_rows, product)

    start_total = jnp.zeros((rep_count, block_rows, feat_width), jnp.float32)
    partials = lax.fori_loop(0, slot_total // group_size, add_group, start_total)
    flat_partials = partials.reshape(rep_count * block_rows, feat_width)
    group_total = lax.psum(flat_partials, "rep")
    own_rows = lax.dynamic_slice_in_dim(
        group_total, lax.axis_index("rep") * block_rows, block_rows, 0
    )
    grad_agg = (inv_sqrt * own_rows).astype(jnp.bfloat16)
    grad_features = lax.dot_general(
        grad_agg, weight, (((1,), (1,)), ((), ())), preferred_element_type=jnp.float32
    ).astype(jnp.bfloat16)
    local_weight = lax.dot_general(
        features, grad_agg, (((0,), (0,)), ((), ())), preferred_element_type=jnp.float32
    )
    grad_weight = lax.psum(local_weight, ("row", "rep"))
    return (grad_features, grad_weight)


def solution(mesh):
    in_specs = (
        P(("row", "rep"), None),
        P(("row", "rep"), None),
        P(("row", "rep"), None),
        P(),
        P("row", "rep", None, None, None),
        P("row", "rep", None),
        P("row", "rep", None),
        P("row", "rep"),
        P(("row", "rep")),
    )
    out_specs = (P(("row", "rep"), None), P())
    return jax.shard_map(
        per_device, mesh=mesh, in_specs=in_specs, out_specs=out_specs, check_vma=False
    )
```

profile of v0, /device:TPU:1, one launch (start us, length us, event | category | flops | bytes accessed | tf_op | source)
XLA Modules:
  0.0 799.1 jit_solution(445123840008618199)
XLA Ops:
  7.2 0.0 copy-start
  7.2 0.0 all-gather.2.cloned.1.call-start
  7.2 0.7 convert_rsqrt_fusion
  7.9 1.6 fusion.21
  9.5 0.0 all-gather.2.cloned.1.call-update
  9.5 0.0 all-reduce.3.cloned.1.call-start
  10.2 0.7 fusion.23
  10.9 216.1 %all-gather.2.cloned.1.call-done = bf16[16384,256]{1,0:T(8,128)(2,1)} async-done(((bf16[128,256]{1,0:T(8,128)(2,1)}), bf16[16384,256]{1,0:T(8,128)(2,1)}) %all-gather.2.cloned.1.call-update) | async-done | bytes 8388624 | tf_op jit(solution)/shard_map/all_gather | solution.py:19
  227.1 21.8 %while.14 = (s32[]{:T(128)}, f32[4,128,256]{2,0,1:T(4,128)S(1)}, bf16[48,4]{0,1:T(4,128)(2,1)S(1)}, bf16[48,128,128]{2,1,0:T(8,128)(2,1)}, s32[48]{0:T(128)}, /*...) while((s32[]{:T(128)}, f32[4,128,256]{2,0,1:T(4,128)S(1)}, ...), condition=%wide.region_1.0_spmd.clone, body=%wide.region_0.1_spmd.clone.sunk | while | flops 139199584 | bytes 6820681 | solution.py:42
  227.1 0.7 compare_and_fusion.2
  227.8 4.0 gather_fusion
  231.8 1.6 fusion.36
  233.4 1.0 fusion.37
  234.3 0.7 compare_and_fusion.2
  235.1 4.0 gather_fusion
  239.1 1.6 fusion.36
  240.7 1.0 fusion.37
  241.6 0.7 compare_and_fusion.2
  242.4 4.0 gather_fusion
  246.4 1.6 fusion.36
  247.9 1.0 fusion.37
  248.9 0.0 copy-start.1
  248.9 0.9 copy.12
  249.8 0.0 all-reduce.3.cloned.1.call-update
  249.8 0.0 all-reduce.5.cloned.1.call-start
  249.9 84.1 %all-reduce.3.cloned.1.call-done = f32[512,256]{1,0:T(8,128)} async-done(((f32[512,256]{1,0:T(8,128)}), f32[512,256]{1,0:T(8,128)}) %all-reduce.3.cloned.1.call-update) | async-done | bytes 524304 | tf_op jit(solution)/shard_map/psum | solution.py:44
  334.0 0.0 copy-done.1
  334.0 1.9 convolution_bitcast_fusion
  335.8 0.0 all-reduce.5.cloned.1.call-update
  335.9 1.8 convolution_convert_fusion
  337.6 453.2 %all-reduce.5.cloned.1.call-done = f32[256,256]{0,1:T(8,128)} async-done(((f32[256,256]{0,1:T(8,128)}), f32[256,256]{0,1:T(8,128)}) %all-reduce.5.cloned.1.call-update) | async-done | bytes 262160 | tf_op jit(solution)/shard_map/psum | solution.py:55
  790.8 1.8 copy.13
  (6 shorter events, 0.0 us)
Async XLA Ops:
  7.2 328.7 %copy-start = (bf16[256,256]{1,0:T(8,128)(2,1)S(1)}, bf16[256,256]{1,0:T(8,128)(2,1)}, u32[]{:S(2)}) copy-start(bf16[256,256]{1,0:T(8,128)(2,1)} %param.14) | copy-start | bytes 393220
  7.2 219.9 %all-gather.2.cloned.1.call-start = ((), (), s32[]{:S(2)}) async-start(), calls=%async_computation | async-start | bytes 8454144 | tf_op jit(solution)/shard_map/all_gather | solution.py:19
  9.5 324.4 %all-reduce.3.cloned.1.call-start = ((), (), s32[]{:S(2)}) async-start(), calls=%async_computation.1 | async-start | bytes 1048576 | tf_op jit(solution)/shard_map/psum | solution.py:44
  248.9 85.1 %copy-start.1 = (bf16[128,256]{1,0:T(8,128)(2,1)S(1)}, bf16[128,256]{1,0:T(8,128)(2,1)}, u32[]{:S(2)}) copy-start(bf16[128,256]{1,0:T(8,128)(2,1)} %param.13) | copy-start | bytes 196612
  249.8 541.0 %all-reduce.5.cloned.1.call-start = ((), (), s32[]{:S(2)}) async-start(), calls=%async_computation.2 | async-start | bytes 524288 | tf_op jit(solution)/shard_map/psum | solution.py:55
Sparse Core Ops, SparseCore 0:
  10.7 216.2 all-gather.1
  249.9 83.9 all-reduce.2
  340.0 450.7 all-reduce.4
where the time goes:
time: 800 us; the launch traced here: 799 us
  waiting for transfers between devices  753 us (94%)
  local copies, waits for them, and re-layouts  14.7 us (2%)
  between operations  14.4 us (2%)
  matrix products  11.2 us (1%)
    psum x1, waiting for transfers between devices, per_device(): grad_weight = lax.psum(local_weight, ('row', 'rep'))  453 us
    all_gather x1, waiting for transfers between devices, per_device(): gathered = lax.all_gather(scaled_grad, 'row', axis=0, tiled=True)  216 us
    psum x1, waiting for transfers between devices, per_device(): group_total = lax.psum(flat_partials, 'rep')  84.1 us
  transfers between devices with their start and end apart: 3, of which 3 were waited for; matrix products, arithmetic and copies ran while one was open for 0% of the time, Pallas kernels for 0%

commit v1 on v0

v1 whole, which is shorter than its diff:
```python
import jax
import jax.numpy as jnp
from jax import lax
from jax.experimental import pallas as pl
from jax.experimental.pallas import tpu as pltpu
from jax.sharding import PartitionSpec as P

MESH = pl.DeviceIdType.MESH
BF16 = jnp.bfloat16
F32 = jnp.float32
SLOTS = 48
DIRS = (1, -1)
CLASSES = (0, 1)
DIR_AT = {1: 0, -1: 1}
PIECE_AT = {0: 0, -1: 1, 1: 2, 2: 3}
LAYER_ORDER = [[1, 2, 3], [0, 2, 3], [3, 1, 0], [2, 1, 0]]
LAYER_CODE = sum(
    LAYER_ORDER[z][j] * 4 ** (z * 3 + j) for z in range(4) for j in range(3)
)
STEPS = (
    ("begin", 0), ("stage", 0), ("middle", 0), ("begin", 1), ("stage", 1), ("begin", 2), ("middle", 1),
    ("begin", 3), ("stage", 2), ("middle", 2), ("end", 0), ("middle", 3), ("end", 1), ("finish", 0),
    ("end", 2), ("finish", 1), ("end", 3), ("finish", 2), ("finish", 3),
)


def kernel(
    grad_hbm, pre_hbm, feat_hbm, weight_hbm, tiles_hbm, rows_ref, cols_ref, count_ref,
    degrees_ref, gf_out, gw_out,
    G, grad_v, pre_v, feat_v, weight_v, tiles_v, stacked, total, feat_t, part16, part_in,
    w16, w_in1, w_in2, w_in3,
    load_sem, z_send, z_recv, s1_send, s1_recv, s2_send, s2_recv, s3_send, s3_recv,
    s4_send, s4_recv, sib_send, sib_recv, feat_send, feat_recv, part_send, part_recv,
    w1_send, w1_recv, w2_send, w2_recv, w3_send, w3_recv, ring1, ring2, ring3,
):
    row = lax.axis_index("row")
    rep = lax.axis_index("rep")
    c = row % 2
    y = (row // 2) % 4
    x = (row // 8) % 4
    zl = row // 32
    layer_at = row % 32

    def dev(at_z, at_x, at_y, at_c):
        return (((at_z * 4 + at_x) * 4 + at_y) * 2 + at_c, rep)

    xs = {0: x, 1: (x + 1) % 4, 2: (x + 2) % 4, -1: (x + 3) % 4}
    ys = {0: y, 1: (y + 1) % 4, 2: (y + 2) % 4, -1: (y + 3) % 4}
    near = {
        (0, 1): dev(zl, xs[1], y, c),
        (0, -1): dev(zl, xs[-1], y, c),
        (1, 1): dev(zl, x, ys[1], c),
        (1, -1): dev(zl, x, ys[-1], c),
    }
    sibling = dev(zl, x, y, 1 - c)
    z_mates = [dev((zl + j) % 4, x, y, c) for j in (1, 2, 3)]
    rep_mates = [(row, (rep + j) % 4) for j in (1, 2, 3)]
    far = {0: dev(zl, xs[2], y, c), 1: dev(zl, x, ys[2], c)}
    z_at = rep * 4 + zl

    def ring(step):
        at = (z_at + step + 16) % 16
        return ((at % 4) * 32 + layer_at, at // 4)

    def signal(sem, to):
        pl.semaphore_signal(sem, inc=1, device_id=to, device_id_type=MESH)


    loads = [
        pltpu.make_async_copy(src, dst, load_sem.at[i])
        for i, (src, dst) in enumerate(
            [
                (grad_hbm, grad_v),
                (pre_hbm, pre_v),
                (feat_hbm, feat_v),
                (tiles_hbm, tiles_v),
                (weight_hbm, weight_v),
            ]
        )
    ]
    for load in loads:
        load.start()

    barrier = pltpu.get_barrier_semaphore()
    peers = list(near.values()) + list(far.values()) + [sibling] + z_mates + [ring(1), ring(-1)]
    for peer in peers:
        signal(barrier, peer)

    inv_row = lax.rsqrt(degrees_ref[...].astype(F32))
    inv_half = jnp.broadcast_to(inv_row, (128, 128)).T
    inv = jnp.concatenate([inv_half, inv_half], axis=1)

    loads[0].wait()
    loads[1].wait()
    pre = pre_v[...].astype(F32)
    gate = jax.nn.sigmoid(pre)
    grad_pre = grad_v[...].astype(F32) * gate * (1.0 + pre * (1.0 - gate))
    G[c, zl, x, y] = (inv * grad_pre).astype(BF16)

    pl.semaphore_wait(barrier, len(peers))
    signal(ring1, ring(1))
    signal(ring1, ring(-1))

    sends = []

    def copy(src, dst, send_sem, recv_sem, to):
        return pltpu.make_async_remote_copy(
            src_ref=src,
            dst_ref=dst,
            send_sem=send_sem,
            recv_sem=recv_sem,
            device_id=to,
            device_id_type=MESH,
        )

    def same(ref, send_sem, recv_sem, to):
        return copy(ref, ref, send_sem, recv_sem, to)

    def go(cp):
        cp.start()
        sends.append(cp)

    layers = [zl] + [(LAYER_CODE // 4 ** j // _power(zl)) % 4 for j in range(3)]

    def piece(k, layer, dp, dq, low, size):
        dx, dy = (dp, dq) if k == 0 else (dq, dp)
        return G.at[c, layer, xs[dx], ys[dy], pl.ds(k * 64 + low, size)]

    def first(j, k, d, dp):
        at = (j, k, DIR_AT[d])
        return same(piece(k, layers[j], dp, 0, 0, 64), s1_send.at[at], s1_recv.at[at], near[k, d])

    def first_far(j, k, dp):
        at = (j, k)
        return same(piece(k, layers[j], dp, 0, 0, 64), s2_send.at[at], s2_recv.at[at], far[k])

    def second(j, k, dp, d, dq):
        at = (j, k, PIECE_AT[dp], DIR_AT[d])
        return same(
            piece(k, layers[j], dp, dq, 0, 64), s3_send.at[at], s3_recv.at[at], near[1 - k, d]
        )

    def second_far(j, k, dp, d, dq):
        at = (j, k, PIECE_AT[dp], DIR_AT[d])
        low = 0 if d == 1 else 32
        return same(
            piece(k, layers[j], dp, dq, low, 32), s4_send.at[at], s4_recv.at[at], near[1 - k, d]
        )

    def step_begin(j):
        if j > 0:
            same(G.at[c, layers[j], x, y], z_send.at[0], z_recv.at[layers[j]], sibling).wait_recv()
        for d in DIRS:
            for k in CLASSES:
                go(first(j, k, d, 0))
        for k in CLASSES:
            go(first_far(j, k, 0))
        for d in DIRS:
            for k in CLASSES:
                go(second(j, k, 0, d, 0))

    def step_middle(j):
        for dp in (-1, 1):
            for d in DIRS:
                for k in CLASSES:
                    if d == 1:
                        first(j, k, -dp, dp).wait_recv()
                    go(second(j, k, dp, d, 0))
        for d in DIRS:
            for k in CLASSES:
                if d == 1:
                    first_far(j, k, 2).wait_recv()
                go(second(j, k, 2, d, 0))

    def step_end(j):
        for dp in (0, -1, 1, 2):
            for d in DIRS:
                for k in CLASSES:
                    second(j, k, dp, d, -d).wait_recv()
                    go(second_far(j, k, dp, d, -d))

    def to_sibling(ref, at):
        return same(ref, sib_send.at[at], sib_recv.at[at], sibling)

    def last_part(core, k, dp):
        if k == 0:
            return G.at[core, layers[3], xs[dp], :, pl.ds(0, 64)]
        return G.at[core, layers[3], :, ys[dp], pl.ds(64, 64)]

    def step_finish(j):
        for dp in (0, -1, 1, 2):
            for k in CLASSES:
                for d in DIRS:
                    second_far(j, k, dp, d, 2).wait_recv()
                if j == 3:
                    go(to_sibling(last_part(c, k, dp), 3 + 4 * k + PIECE_AT[dp]))
        if j < 3:
            go(to_sibling(G.at[c, layers[j]], j))

    mine = G.at[c, zl, x, y]
    for j, mate in enumerate(z_mates):
        go(same(mine, z_send.at[j], z_recv.at[zl], mate))

    step_begin(0)

    loads[2].wait()
    feat_t[rep] = (inv * feat_v[...].astype(F32)).T.astype(BF16)

    loads[3].wait()
    count = count_ref[0, 0]

    def spread(i, carry):
        for n in range(4):
            tile = tiles_v[i * 4 + n]
            live = i * 4 + n < count
            at = rows_ref[0, i * 4 + n]
            for r in range(4):
                stacked[r, i, :, pl.ds(n * 128, 128)] = jnp.where(
                    jnp.logical_and(live, at == r), tile, jnp.zeros_like(tile)
                )
        return carry

    lax.fori_loop(0, SLOTS // 4, spread, 0)

    def step_stage(n):
        if n == 0:
            pl.semaphore_wait(ring1, 2)
            signal(ring2, ring(2))
            signal(ring2, ring(-2))
        elif n == 1:
            pl.semaphore_wait(ring2, 2)
            signal(ring3, ring(4))
            signal(ring3, ring(-4))
        else:
            pl.semaphore_wait(ring3, 2)
            for j, mate in enumerate(rep_mates):
                go(same(feat_t.at[rep], feat_send.at[j], feat_recv.at[rep], mate))

    steps = {
        "begin": step_begin, "middle": step_middle, "end": step_end, "finish": step_finish,
        "stage": step_stage,
    }
    for name, j in STEPS[1:]:
        steps[name](j)
    for j in range(3):
        to_sibling(G.at[1 - c, layers[j]], j).wait_recv()
    for dp in (0, -1, 1, 2):
        for k in CLASSES:
            to_sibling(last_part(1 - c, k, dp), 3 + 4 * k + PIECE_AT[dp]).wait_recv()

    def block(s):
        col = cols_ref[0, s]
        return G[col % 2, col // 32, (col // 8) % 4, (col // 2) % 4]

    def multiply(r):
        def add(i, acc):
            right = jnp.concatenate([block(i * 4 + n) for n in range(4)], axis=0)
            return acc + jnp.dot(stacked[r, i], right, preferred_element_type=F32)

        return lax.fori_loop(0, SLOTS // 4, add, jnp.zeros((128, 256), F32))

    gather_sends = list(sends)
    sends.clear()
    for j in (2, 1, 3):
        to = (rep + j) % 4
        part16[to] = multiply(to).astype(BF16)
        go(copy(part16.at[to], part_in.at[rep], part_send.at[j - 1], part_recv.at[rep], (row, to)))
    total[...] = multiply(rep)
    part16[rep] = total[...].astype(BF16)

    for j in (1, 2, 3):
        other = (rep + j) % 4
        same(feat_t.at[other], feat_send.at[0], feat_recv.at[other], sibling).wait_recv()
    term16 = jnp.dot(
        jnp.concatenate([feat_t[r] for r in range(4)], axis=1),
        jnp.concatenate([part16[r] for r in range(4)], axis=0),
        preferred_element_type=F32,
    ).astype(BF16)
    w16[0:16] = term16[:, 0:128].reshape(16, 16, 128)
    w16[16:32] = term16[:, 128:256].reshape(16, 16, 128)

    def wait_all(ref, count, sem):
        part = ref.at[pl.ds(0, count)]
        pltpu.make_async_copy(part, part, sem).wait()

    for j in range(1, 32):
        to = (layer_at + j) % 32
        copy(w16.at[to], w_in1.at[layer_at], w1_send, w1_recv, (zl * 32 + to, rep)).start()
    w_in1[layer_at] = w16[layer_at]
    for cp in gather_sends:
        cp.wait_send()
    wait_all(w_in1, 31, w1_recv)
    w_in2[z_at] = jnp.sum(w_in1[...].astype(F32), axis=0).astype(BF16)
    for j in range(1, 16):
        copy(w_in2.at[z_at], w_in2.at[z_at], w2_send, w2_recv, ring(j)).start()
    wait_all(w16, 31, w1_send)
    wait_all(w_in2, 15, w2_recv)
    w_in3[layer_at] = jnp.sum(w_in2[...].astype(F32), axis=0).astype(BF16)
    for j in range(1, 32):
        to = (layer_at + j) % 32
        copy(w_in3.at[layer_at], w_in3.at[layer_at], w3_send, w3_recv, (zl * 32 + to, rep)).start()

    for j in (1, 2, 3):
        at = (rep + j) % 4
        copy(part16.at[0], part_in.at[at], part_send.at[0], part_recv.at[at], sibling).wait_recv()
    agg = total[...]
    for j in (1, 2, 3):
        agg += part_in[(rep + j) % 4].astype(F32)
    loads[4].wait()
    gf_out[...] = lax.dot_general(
        (inv * agg).astype(BF16), weight_v[...], (((1,), (1,)), ((), ())),
        preferred_element_type=F32,
    ).astype(BF16)
    for cp in sends:
        cp.wait_send()
    wait_all(w_in2, 15, w2_send)

    wait_all(w_in3, 31, w3_recv)
    gw_out[:, 0:128] = w_in3[0:16].astype(F32).reshape(256, 128)
    gw_out[:, 128:256] = w_in3[16:32].astype(F32).reshape(256, 128)
    wait_all(w_in3, 31, w3_send)


def _power(zl):
    return 1 + (zl >= 1) * 63 + (zl >= 2) * (64 * 63) + (zl >= 3) * (64 * 64 * 63)


def per_device(
    grad_out, pre_act, features, weight, tile_values, tile_rows, tile_cols, tile_count, degrees
):
    dma = pltpu.SemaphoreType.DMA
    regular = pltpu.SemaphoreType.REGULAR
    vmem = pltpu.VMEM
    any_spec = pl.BlockSpec(memory_space=pl.ANY)
    smem_spec = pl.BlockSpec(memory_space=pltpu.SMEM)
    vmem_spec = pl.BlockSpec(memory_space=pltpu.VMEM)
    return pl.pallas_call(
        kernel,
        out_shape=(
            jax.ShapeDtypeStruct((128, 256), BF16),
            jax.ShapeDtypeStruct((256, 256), F32),
        ),
        in_specs=[any_spec] * 5 + [smem_spec] * 3 + [vmem_spec],
        out_specs=(vmem_spec, vmem_spec),
        scratch_shapes=[
            vmem((2, 4, 4, 4, 128, 256), BF16),
            vmem((128, 256), BF16),
            vmem((128, 256), BF16),
            vmem((128, 256), BF16),
            vmem((256, 256), BF16),
            vmem((SLOTS, 128, 128), BF16),
            vmem((4, SLOTS // 4, 128, 512), BF16),
            vmem((128, 256), F32),
            vmem((4, 256, 128), BF16),
            vmem((4, 128, 256), BF16),
            vmem((4, 128, 256), BF16),
            vmem((32, 16, 128), BF16),
            vmem((32, 16, 128), BF16),
            vmem((16, 16, 128), BF16),
            vmem((32, 16, 128), BF16),
            dma((5,)),
            dma((3,)), dma((4,)),
            dma((4, 2, 2)), dma((4, 2, 2)), dma((4, 2)), dma((4, 2)),
            dma((4, 2, 4, 2)), dma((4, 2, 4, 2)), dma((4, 2, 4, 2)), dma((4, 2, 4, 2)),
            dma((11,)), dma((11,)),
            dma((3,)), dma((4,)),
            dma((3,)), dma((4,)),
            dma, dma, dma, dma, dma, dma,
            regular, regular, regular,
        ],
        compiler_params=pltpu.CompilerParams(
            collective_id=0, has_side_effects=True, vmem_limit_bytes=62 * 2**20
        ),
    )(
        grad_out, pre_act, features, weight, tile_values[0, 0],
        tile_rows.reshape(1, SLOTS), tile_cols.reshape(1, SLOTS), tile_count,
        degrees.reshape(1, 128),
    )


def solution(mesh):
    in_specs = (
        P(("row", "rep"), None),
        P(("row", "rep"), None),
        P(("row", "rep"), None),
        P(),
        P("row", "rep", None, None, None),
        P("row", "rep", None),
        P("row", "rep", None),
        P("row", "rep"),
        P(("row", "rep")),
    )
    out_specs = (P(("row", "rep"), None), P())
    return jax.shard_map(
        per_device, mesh=mesh, in_specs=in_specs, out_specs=out_specs, check_vma=False
    )
```

time: 800 us -> 82.5 us (0.10)
  waiting for transfers between devices: 753 us -> 0 us
  Pallas kernels: 0 us -> 77.8 us
  between operations: 14.4 us -> 1.29 us
  local copies, waits for them, and re-layouts: 14.7 us -> 3.14 us
  matrix products: 11.2 us -> 0 us
    psum x2 -> x0, waiting for transfers between devices: 537 us -> none  [the longest x1 453 us: per_device(): grad_weight = lax.psum(local_weight, ('row', 'rep'))]
    all_gather x1 -> x0, waiting for transfers between devices: 216 us -> none  [per_device(): gathered = lax.all_gather(scaled_grad, 'row', axis=0, tiled=True)]
    pallas_call x0 -> x1, Pallas kernels: none -> 77.8 us  [per_device(): pl.pallas_call(kernel, out_shape=(jax.ShapeDtypeStruct((128, 256), BF16),...]
    gather x3 -> x0, local copies, waits for them, and re-layouts: 12 us -> none  [add_group(): picked = jnp.take(column_blocks, group_cols, axis=0)]
    dot_general x8 -> x0, matrix products: 11.2 us -> none  [the longest x3 4.65 us: add_group(): jnp.einsum('sij,sjf->sif', group_tiles, picked, preferred_element_type=jn...]
  transfers between devices with their start and end apart: 3 -> 0, of which waited for: 3 -> 0; matrix products, arithmetic and copies ran while one was open for 0% -> 0% of each run, Pallas kernels for 0% -> 0%
where the time goes in v1:
time: 82.5 us; the launch traced here: 82.2 us
  Pallas kernels  77.8 us (94%)
  local copies, waits for them, and re-layouts  3.14 us (4%)
  between operations  1.29 us (2%)
    pallas_call x1, Pallas kernels, per_device(): pl.pallas_call(kernel, out_shape=(jax.ShapeDtypeStruct((128, 256), BF16),...  77.8 us
    unnamed x2, local copies, waits for them, and re-layouts  3.14 us

profile of v1, /device:TPU:1, one launch (start us, length us, event | category | flops | bytes accessed | tf_op | source)
XLA Modules:
  0.0 82.2 jit_solution(16045355768389874968)
XLA Ops:
  1.3 77.8 %shard_map.104 = (bf16[128,256]{1,0:T(8,128)(2,1)}, f32[256,256]{1,0:T(8,128)}) custom-call(bf16[128,256]{1,0:T(8,128)(2,1)} %grad_hbm.1, bf16[128,256]{1,0:T(8,128)(2,1)} %pre_hbm.1, bf16[128,256]{1,0:T(8,128)(2,1)} %feat_hbm.1, bf16[256,256]{1,0:T(8,128)(2,1)} %weight_hbm.1, bf16[48,128,128]{2,1,0:T(8,128)(2,1)} %bitcast.4, s32[1,48]{1,0:T(1,128)} %bitcast.5, ...), custom_call_target="tpu_custom_call" | custom-call | tf_op jit(solution)/shard_map/pallas_call | solution.py:337
  79.1 1.5 %copy.14 = bf16[128,256]{1,0:T(8,128)(2,1)} copy(bf16[128,256]{1,0:T(8,128)(2,1)} %get-tuple-element.4) | data formatting | bytes 131072
  80.6 1.7 %copy.15 = f32[256,256]{1,0:T(8,128)} copy(f32[256,256]{1,0:T(8,128)} %get-tuple-element.5) | data formatting | bytes 524288

commit v2 on v1

--- a/solution.py
+++ b/solution.py
@@ -9,6 +9,7 @@
 BF16 = jnp.bfloat16
 F32 = jnp.float32
 SLOTS = 48
+EARLY = 0
 DIRS = (1, -1)
 CLASSES = (0, 1)
 DIR_AT = {1: 0, -1: 1}
@@ -27,7 +28,7 @@
 def kernel(
     grad_hbm, pre_hbm, feat_hbm, weight_hbm, tiles_hbm, rows_ref, cols_ref, count_ref,
     degrees_ref, gf_out, gw_out,
-    G, grad_v, pre_v, feat_v, weight_v, tiles_v, stacked, total, feat_t, part16, part_in,
+    G, grad_v, pre_v, feat_v, weight_v, tiles_v, stacked, picked, total, feat_t, part16, part_in,
     w16, w_in1, w_in2, w_in3,
     load_sem, z_send, z_recv, s1_send, s1_recv, s2_send, s2_recv, s3_send, s3_recv,
     s4_send, s4_recv, sib_send, sib_recv, feat_send, feat_recv, part_send, part_recv,
@@ -171,6 +172,8 @@
                 if d == 1:
                     first_far(j, k, 2).wait_recv()
                 go(second(j, k, 2, d, 0))
+        for k in CLASSES:
+            go(to_sibling(c, j, k, 0))
 
     def step_end(j):
         for dp in (0, -1, 1, 2):
@@ -178,24 +181,24 @@
                 for k in CLASSES:
                     second(j, k, dp, d, -d).wait_recv()
                     go(second_far(j, k, dp, d, -d))
-
-    def to_sibling(ref, at):
+        for d in DIRS:
+            for k in CLASSES:
+                go(to_sibling(c, j, k, d))
+
+    def to_sibling(core, j, k, dq):
+        if k == 0:
+            ref = G.at[core, layers[j], :, ys[dq], pl.ds(0, 64)]
+        else:
+            ref = G.at[core, layers[j], xs[dq], :, pl.ds(64, 64)]
+        at = (j, k, PIECE_AT[dq])
         return same(ref, sib_send.at[at], sib_recv.at[at], sibling)
 
-    def last_part(core, k, dp):
-        if k == 0:
-            return G.at[core, layers[3], xs[dp], :, pl.ds(0, 64)]
-        return G.at[core, layers[3], :, ys[dp], pl.ds(64, 64)]
-
     def step_finish(j):
-        for dp in (0, -1, 1, 2):
-            for k in CLASSES:
+        for k in CLASSES:
+            for dp in (0, -1, 1, 2):
                 for d in DIRS:
                     second_far(j, k, dp, d, 2).wait_recv()
-                if j == 3:
-                    go(to_sibling(last_part(c, k, dp), 3 + 4 * k + PIECE_AT[dp]))
-        if j < 3:
-            go(to_sibling(G.at[c, layers[j]], j))
+            go(to_sibling(c, j, k, 2))
 
     mine = G.at[c, zl, x, y]
     for j, mate in enumerate(z_mates):
@@ -209,18 +212,17 @@
     loads[3].wait()
     count = count_ref[0, 0]
 
-    def spread(i, carry):
-        for n in range(4):
-            tile = tiles_v[i * 4 + n]
-            live = i * 4 + n < count
-            at = rows_ref[0, i * 4 + n]
-            for r in range(4):
-                stacked[r, i, :, pl.ds(n * 128, 128)] = jnp.where(
-                    jnp.logical_and(live, at == r), tile, jnp.zeros_like(tile)
-                )
+    def spread(s, carry):
+        tile = tiles_v[s]
+        live = s < count
+        at = rows_ref[0, s]
+        for r in range(4):
+            stacked[r, :, pl.ds(pl.multiple_of(s * 128, 128), 128)] = jnp.where(
+                jnp.logical_and(live, at == r), tile, jnp.zeros_like(tile)
+            )
         return carry
 
-    lax.fori_loop(0, SLOTS // 4, spread, 0)
+    lax.fori_loop(0, SLOTS, spread, 0)
 
     def step_stage(n):
         if n == 0:
@@ -242,22 +244,17 @@
     }
     for name, j in STEPS[1:]:
         steps[name](j)
-    for j in range(3):
-        to_sibling(G.at[1 - c, layers[j]], j).wait_recv()
-    for dp in (0, -1, 1, 2):
+    for j in range(4):
         for k in CLASSES:
-            to_sibling(last_part(1 - c, k, dp), 3 + 4 * k + PIECE_AT[dp]).wait_recv()
-
-    def block(s):
+            for dq in (0, -1, 1, 2):
+                to_sibling(1 - c, j, k, dq).wait_recv()
+
+    for s in range(SLOTS):
         col = cols_ref[0, s]
-        return G[col % 2, col // 32, (col // 8) % 4, (col // 2) % 4]
+        picked[pl.ds(s * 128, 128), :] = G[col % 2, col // 32, (col // 8) % 4, (col // 2) % 4]
 
     def multiply(r):
-        def add(i, acc):
-            right = jnp.concatenate([block(i * 4 + n) for n in range(4)], axis=0)
-            return acc + jnp.dot(stacked[r, i], right, preferred_element_type=F32)
-
-        return lax.fori_loop(0, SLOTS // 4, add, jnp.zeros((128, 256), F32))
+        return jnp.dot(stacked[r], picked[...], preferred_element_type=F32)
 
     gather_sends = list(sends)
     sends.clear()
@@ -287,13 +284,15 @@
         to = (layer_at + j) % 32
         copy(w16.at[to], w_in1.at[layer_at], w1_send, w1_recv, (zl * 32 + to, rep)).start()
     w_in1[layer_at] = w16[layer_at]
-    for cp in gather_sends:
+    for cp in gather_sends[:EARLY]:
         cp.wait_send()
     wait_all(w_in1, 31, w1_recv)
     w_in2[z_at] = jnp.sum(w_in1[...].astype(F32), axis=0).astype(BF16)
     for j in range(1, 16):
         copy(w_in2.at[z_at], w_in2.at[z_at], w2_send, w2_recv, ring(j)).start()
     wait_all(w16, 31, w1_send)
+    for cp in gather_sends[EARLY:]:
+        cp.wait_send()
     wait_all(w_in2, 15, w2_recv)
     w_in3[layer_at] = jnp.sum(w_in2[...].astype(F32), axis=0).astype(BF16)
     for j in range(1, 32):
@@ -349,7 +348,8 @@
             vmem((128, 256), BF16),
             vmem((256, 256), BF16),
             vmem((SLOTS, 128, 128), BF16),
-            vmem((4, SLOTS // 4, 128, 512), BF16),
+            vmem((4, 128, SLOTS * 128), BF16),
+            vmem((SLOTS * 128, 256), BF16),
             vmem((128, 256), F32),
             vmem((4, 256, 128), BF16),
             vmem((4, 128, 256), BF16),
@@ -362,7 +362,7 @@
             dma((3,)), dma((4,)),
             dma((4, 2, 2)), dma((4, 2, 2)), dma((4, 2)), dma((4, 2)),
             dma((4, 2, 4, 2)), dma((4, 2, 4, 2)), dma((4, 2, 4, 2)), dma((4, 2, 4, 2)),
-            dma((11,)), dma((11,)),
+            dma((4, 2, 4)), dma((4, 2, 4)),
             dma((3,)), dma((4,)),
             dma((3,)), dma((4,)),
             dma, dma, dma, dma, dma, dma,

time: 82.5 us -> 77.4 us (0.938)
  Pallas kernels: 77.8 us -> 72.7 us
    pallas_call x1, Pallas kernels: 77.8 us -> 72.7 us  [per_device(): pl.pallas_call(kernel, out_shape=(jax.ShapeDtypeStruct((128, 256), BF16),...]
where the time goes in v2:
time: 77.4 us; the launch traced here: 77.2 us
  Pallas kernels  72.7 us (94%)
  local copies, waits for them, and re-layouts  3.14 us (4%)
  between operations  1.29 us (2%)
    pallas_call x1, Pallas kernels, per_device(): pl.pallas_call(kernel, out_shape=(jax.ShapeDtypeStruct((128, 256), BF16),...  72.7 us
    unnamed x2, local copies, waits for them, and re-layouts  3.14 us

profile of v2, /device:TPU:1, one launch (start us, length us, event | category | flops | bytes accessed | tf_op | source)
XLA Modules:
  0.0 77.2 jit_solution(11072187261477333401)
XLA Ops:
  1.3 72.7 %shard_map.104 = (bf16[128,256]{1,0:T(8,128)(2,1)}, f32[256,256]{1,0:T(8,128)}) custom-call(bf16[128,256]{1,0:T(8,128)(2,1)} %grad_hbm.1, bf16[128,256]{1,0:T(8,128)(2,1)} %pre_hbm.1, bf16[128,256]{1,0:T(8,128)(2,1)} %feat_hbm.1, bf16[256,256]{1,0:T(8,128)(2,1)} %weight_hbm.1, bf16[48,128,128]{2,1,0:T(8,128)(2,1)} %bitcast.4, s32[1,48]{1,0:T(1,128)} %bitcast.5, ...), custom_call_target="tpu_custom_call" | custom-call | tf_op jit(solution)/shard_map/pallas_call | solution.py:336
  74.0 1.5 %copy.14 = bf16[128,256]{1,0:T(8,128)(2,1)} copy(bf16[128,256]{1,0:T(8,128)(2,1)} %get-tuple-element.4) | data formatting | bytes 131072
  75.5 1.7 %copy.15 = f32[256,256]{1,0:T(8,128)} copy(f32[256,256]{1,0:T(8,128)} %get-tuple-element.5) | data formatting | bytes 524288

commit v3 on v2

--- a/solution.py
+++ b/solution.py
@@ -9,7 +9,11 @@
 BF16 = jnp.bfloat16
 F32 = jnp.float32
 SLOTS = 48
-EARLY = 0
+LAYER_OFFSETS = sorted(
+    [(dx, dy, dc) for dx in (2, 1, -1, 0) for dy in (2, 1, -1, 0) for dc in (0, 1)],
+    key=lambda at: -(abs(at[0]) + abs(at[1]) + at[2] / 2),
+)[:-1]
+RING_STEPS = sorted(range(1, 16), key=lambda j: -min(j, 16 - j))
 DIRS = (1, -1)
 CLASSES = (0, 1)
 DIR_AT = {1: 0, -1: 1}
@@ -26,9 +30,9 @@
 
 
 def kernel(
-    grad_hbm, pre_hbm, feat_hbm, weight_hbm, tiles_hbm, rows_ref, cols_ref, count_ref,
-    degrees_ref, gf_out, gw_out,
-    G, grad_v, pre_v, feat_v, weight_v, tiles_v, stacked, picked, total, feat_t, part16, part_in,
+    grad_hbm, pre_hbm, feat_hbm, weight_hbm, tiles_hbm, rows_hbm, cols_hbm, count_hbm,
+    degrees_hbm, gf_out, gw_out,
+    rows_ref, cols_ref, count_ref, degrees_ref, G, grad_v, pre_v, feat_v, weight_v, tiles_v, stacked, picked, total, feat_t, part16, part_in,
     w16, w_in1, w_in2, w_in3,
     load_sem, z_send, z_recv, s1_send, s1_recv, s2_send, s2_recv, s3_send, s3_recv,
     s4_send, s4_recv, sib_send, sib_recv, feat_send, feat_recv, part_send, part_recv,
@@ -76,6 +80,10 @@
                 (feat_hbm, feat_v),
                 (tiles_hbm, tiles_v),
                 (weight_hbm, weight_v),
+                (degrees_hbm, degrees_ref),
+                (rows_hbm, rows_ref),
+                (cols_hbm, cols_ref),
+                (count_hbm, count_ref),
             ]
         )
     ]
@@ -87,6 +95,7 @@
     for peer in peers:
         signal(barrier, peer)
 
+    loads[5].wait()
     inv_row = lax.rsqrt(degrees_ref[...].astype(F32))
     inv_half = jnp.broadcast_to(inv_row, (128, 128)).T
     inv = jnp.concatenate([inv_half, inv_half], axis=1)
@@ -210,6 +219,8 @@
     feat_t[rep] = (inv * feat_v[...].astype(F32)).T.astype(BF16)
 
     loads[3].wait()
+    for load in loads[6:]:
+        load.wait()
     count = count_ref[0, 0]
 
     def spread(s, carry):
@@ -256,12 +267,17 @@
     def multiply(r):
         return jnp.dot(stacked[r], picked[...], preferred_element_type=F32)
 
+    def part_to(j):
+        to = (rep + j) % 4
+        return copy(part16.at[to], part_in.at[rep], part_send.at[j - 1], part_recv.at[rep], (row, to))
+
     gather_sends = list(sends)
     sends.clear()
     for j in (2, 1, 3):
         to = (rep + j) % 4
         part16[to] = multiply(to).astype(BF16)
-        go(copy(part16.at[to], part_in.at[rep], part_send.at[j - 1], part_recv.at[rep], (row, to)))
+        if j != 2:
+            go(part_to(j))
     total[...] = multiply(rep)
     part16[rep] = total[...].astype(BF16)
 
@@ -280,23 +296,21 @@
         part = ref.at[pl.ds(0, count)]
         pltpu.make_async_copy(part, part, sem).wait()
 
-    for j in range(1, 32):
-        to = (layer_at + j) % 32
+    layer_mates = [xs[dx] * 8 + ys[dy] * 2 + (1 - c if dc else c) for dx, dy, dc in LAYER_OFFSETS]
+    for to in layer_mates:
         copy(w16.at[to], w_in1.at[layer_at], w1_send, w1_recv, (zl * 32 + to, rep)).start()
     w_in1[layer_at] = w16[layer_at]
-    for cp in gather_sends[:EARLY]:
-        cp.wait_send()
     wait_all(w_in1, 31, w1_recv)
     w_in2[z_at] = jnp.sum(w_in1[...].astype(F32), axis=0).astype(BF16)
-    for j in range(1, 16):
+    for j in RING_STEPS:
         copy(w_in2.at[z_at], w_in2.at[z_at], w2_send, w2_recv, ring(j)).start()
+    go(part_to(2))
     wait_all(w16, 31, w1_send)
-    for cp in gather_sends[EARLY:]:
+    for cp in gather_sends:
         cp.wait_send()
     wait_all(w_in2, 15, w2_recv)
     w_in3[layer_at] = jnp.sum(w_in2[...].astype(F32), axis=0).astype(BF16)
-    for j in range(1, 32):
-        to = (layer_at + j) % 32
+    for to in layer_mates:
         copy(w_in3.at[layer_at], w_in3.at[layer_at], w3_send, w3_recv, (zl * 32 + to, rep)).start()
 
     for j in (1, 2, 3):
@@ -331,7 +345,6 @@
     regular = pltpu.SemaphoreType.REGULAR
     vmem = pltpu.VMEM
     any_spec = pl.BlockSpec(memory_space=pl.ANY)
-    smem_spec = pl.BlockSpec(memory_space=pltpu.SMEM)
     vmem_spec = pl.BlockSpec(memory_space=pltpu.VMEM)
     return pl.pallas_call(
         kernel,
@@ -339,9 +352,13 @@
             jax.ShapeDtypeStruct((128, 256), BF16),
             jax.ShapeDtypeStruct((256, 256), F32),
         ),
-        in_specs=[any_spec] * 5 + [smem_spec] * 3 + [vmem_spec],
+        in_specs=[any_spec] * 9,
         out_specs=(vmem_spec, vmem_spec),
         scratch_shapes=[
+            pltpu.SMEM((1, SLOTS), jnp.int32),
+            pltpu.SMEM((1, SLOTS), jnp.int32),
+            pltpu.SMEM((1, 1), jnp.int32),
+            vmem((1, 128), jnp.int32),
             vmem((2, 4, 4, 4, 128, 256), BF16),
             vmem((128, 256), BF16),
             vmem((128, 256), BF16),
@@ -358,7 +375,7 @@
             vmem((32, 16, 128), BF16),
             vmem((16, 16, 128), BF16),
             vmem((32, 16, 128), BF16),
-            dma((5,)),
+            dma((9,)),
             dma((3,)), dma((4,)),
             dma((4, 2, 2)), dma((4, 2, 2)), dma((4, 2)), dma((4, 2)),
             dma((4, 2, 4, 2)), dma((4, 2, 4, 2)), dma((4, 2, 4, 2)), dma((4, 2, 4, 2)),

time: 77.4 us -> 74.6 us (0.964)
  Pallas kernels: 72.7 us -> 70 us
    pallas_call x1, Pallas kernels: 72.7 us -> 70 us  [per_device(): pl.pallas_call(kernel, out_shape=(jax.ShapeDtypeStruct((128, 256), BF16),...]
where the time goes in v3:
time: 74.6 us; the launch traced here: 74.4 us
  Pallas kernels  70 us (94%)
  local copies, waits for them, and re-layouts  3.14 us (4%)
  between operations  1.29 us (2%)
    pallas_call x1, Pallas kernels, per_device(): pl.pallas_call(kernel, out_shape=(jax.ShapeDtypeStruct((128, 256), BF16),...  70 us
    unnamed x2, local copies, waits for them, and re-layouts  3.14 us

profile of v3, /device:TPU:1, one launch (start us, length us, event | category | flops | bytes accessed | tf_op | source)
XLA Modules:
  0.0 74.4 jit_solution(10279595338005991517)
XLA Ops:
  1.3 70.0 %shard_map.104 = (bf16[128,256]{1,0:T(8,128)(2,1)}, f32[256,256]{1,0:T(8,128)}) custom-call(bf16[128,256]{1,0:T(8,128)(2,1)} %grad_hbm.1, bf16[128,256]{1,0:T(8,128)(2,1)} %pre_hbm.1, bf16[128,256]{1,0:T(8,128)(2,1)} %feat_hbm.1, bf16[256,256]{1,0:T(8,128)(2,1)} %weight_hbm.1, bf16[48,128,128]{2,1,0:T(8,128)(2,1)} %bitcast.4, s32[1,48]{1,0:T(1,128)} %bitcast.5, ...), custom_call_target="tpu_custom_call" | custom-call | tf_op jit(solution)/shard_map/pallas_call | solution.py:349
  71.3 1.5 %copy.14 = bf16[128,256]{1,0:T(8,128)(2,1)} copy(bf16[128,256]{1,0:T(8,128)(2,1)} %get-tuple-element.4) | data formatting | bytes 131072
  72.7 1.7 %copy.15 = f32[256,256]{1,0:T(8,128)} copy(f32[256,256]{1,0:T(8,128)} %get-tuple-element.5) | data formatting | bytes 524288

commit v4 on v3

--- a/solution.py
+++ b/solution.py
@@ -24,8 +24,8 @@
 )
 STEPS = (
     ("begin", 0), ("stage", 0), ("middle", 0), ("begin", 1), ("stage", 1), ("begin", 2), ("middle", 1),
-    ("begin", 3), ("stage", 2), ("middle", 2), ("end", 0), ("middle", 3), ("end", 1), ("finish", 0),
-    ("end", 2), ("finish", 1), ("end", 3), ("finish", 2), ("finish", 3),
+    ("begin", 3), ("stage", 2), ("middle", 2), ("end", 0), ("middle", 3), ("end", 1), ("end", 2),
+    ("finish", 0), ("end", 3), ("finish", 1), ("finish", 2), ("finish", 3),
 )
 
 

time: 74.6 us -> 73.2 us (0.981)
  Pallas kernels: 70 us -> 68.5 us
    pallas_call x1, Pallas kernels: 70 us -> 68.5 us  [per_device(): pl.pallas_call(kernel, out_shape=(jax.ShapeDtypeStruct((128, 256), BF16),...]
where the time goes in v4:
time: 73.2 us; the launch traced here: 73 us
  Pallas kernels  68.5 us (94%)
  local copies, waits for them, and re-layouts  3.14 us (4%)
  between operations  1.29 us (2%)
    pallas_call x1, Pallas kernels, per_device(): pl.pallas_call(kernel, out_shape=(jax.ShapeDtypeStruct((128, 256), BF16),...  68.5 us
    unnamed x2, local copies, waits for them, and re-layouts  3.14 us

profile of v4, /device:TPU:1, one launch (start us, length us, event | category | flops | bytes accessed | tf_op | source)
XLA Modules:
  0.0 73.0 jit_solution(1697369058868205283)
XLA Ops:
  1.3 68.5 %shard_map.104 = (bf16[128,256]{1,0:T(8,128)(2,1)}, f32[256,256]{1,0:T(8,128)}) custom-call(bf16[128,256]{1,0:T(8,128)(2,1)} %grad_hbm.1, bf16[128,256]{1,0:T(8,128)(2,1)} %pre_hbm.1, bf16[128,256]{1,0:T(8,128)(2,1)} %feat_hbm.1, bf16[256,256]{1,0:T(8,128)(2,1)} %weight_hbm.1, bf16[48,128,128]{2,1,0:T(8,128)(2,1)} %bitcast.4, s32[1,48]{1,0:T(1,128)} %bitcast.5, ...), custom_call_target="tpu_custom_call" | custom-call | tf_op jit(solution)/shard_map/pallas_call | solution.py:349
  69.8 1.5 %copy.14 = bf16[128,256]{1,0:T(8,128)(2,1)} copy(bf16[128,256]{1,0:T(8,128)(2,1)} %get-tuple-element.4) | data formatting | bytes 131072
  71.3 1.7 %copy.15 = f32[256,256]{1,0:T(8,128)} copy(f32[256,256]{1,0:T(8,128)} %get-tuple-element.5) | data formatting | bytes 524288
